TPU v7x, 32 devices: a whole 2x2x4 slice. The times are simulated.
32 devices in a mesh: rep: 2 (over y), gx: 4 (over z), gy: 2 (over x), gz: 2 (over core).
Axes of the slice: x: 2, y: 2, z: 4, core: 2. Of those that a mesh axis runs over, the one named last changes fastest.
Arguments:
- tokens: bfloat16 [1024, 8192], P('rep', ('gx', 'gy', 'gz')), parts along dimension 0, may hold values from -6 to 6
- gate_weight: bfloat16 [8192, 26624], P('gx', ('gy', 'gz')), may hold values from -0.0625 to 0.0625
- up_weight: bfloat16 [8192, 26624], P('gx', ('gy', 'gz')), may hold values from -0.0625 to 0.0625
- down_weight: bfloat16 [26624, 8192], P(('gy', 'gz'), 'gx'), may hold values from -0.0546875 to 0.0546875
Outputs:
- ffn_output: bfloat16 [1024, 8192], P('rep', ('gx', 'gy', 'gz')), parts along dimension 0
There are 2 independent parts, one for each index of `rep`. A program takes and returns all parts, laid end to end along the dimension named above; an argument that names none is the same for every part. Nothing has to cross between parts.
All inputs are finite; a program needn't handle non-finite values.
Results may differ from a plain program's by a relative error of at most 0.019.
Values may be sent and summed in bfloat16 or wider, within the bound.
A program may use at most 256 MiB of HBM per device.

v0:
```python
import jax
import jax.numpy as jnp
from jax import lax
from jax.sharding import PartitionSpec as P


def body(tokens, gate_weight, up_weight, down_weight):
    features = lax.all_gather(tokens, ("gy", "gz"), axis=1, tiled=True)
    gate_sum, up_sum = (
        lax.psum_scatter(
            jnp.dot(features, gate_weight, preferred_element_type=jnp.float32).astype(jnp.bfloat16),
            "gx",
            scatter_dimension=1,
            tiled=True,
        ).astype(jnp.float32),
        lax.psum_scatter(
            jnp.dot(features, up_weight, preferred_element_type=jnp.float32).astype(jnp.bfloat16),
            "gx",
            scatter_dimension=1,
            tiled=True,
        ).astype(jnp.float32),
    )
    hidden = (jax.nn.silu(gate_sum) * up_sum).astype(jnp.bfloat16)
    projected = jnp.dot(
        lax.all_gather(hidden, "gx", axis=1, tiled=True),
        down_weight,
        preferred_element_type=jnp.float32,
    )
    return lax.psum_scatter(
        projected.astype(jnp.bfloat16), ("gy", "gz"), scatter_dimension=1, tiled=True
    )


def solution(mesh):
    placed = (
        P("rep", ("gx", "gy", "gz")),
        P("gx", ("gy", "gz")),
        P("gx", ("gy", "gz")),
        P(("gy", "gz"), "gx"),
    )
    return jax.shard_map(
        body, mesh=mesh, in_specs=placed, out_specs=P("rep", ("gx", "gy", "gz")), check_vma=False
    )
```

profile of v0, /device:TPU:0, one launch (start us, length us, event | category | flops | bytes accessed | tf_op | source)
XLA Modules:
  0.0 495.6 jit_solution(8216409531942160205)
XLA Ops:
  6.5 0.0 all-gather.3.cloned.1.call-start
  6.5 0.7 all-gather.3.cloned.1.call-update
  7.3 0.0 reduce-scatter.12.cloned.1.call-start
  7.3 26.9 %all-gather.3.cloned.1.call-done = bf16[512,2048]{1,0:T(8,128)(2,1)} async-done(((bf16[512,512]{1,0:T(8,128)(2,1)}), bf16[512,2048]{1,0:T(8,128)(2,1)}) %all-gather.3.cloned.1.call-update) | async-done | bytes 2097168 | tf_op jit(solution)/shard_map/all_gather | solution.py:8
  34.2 21.7 %convolution_convert_fusion = bf16[512,6656]{1,0:T(8,128)(2,1)} fusion(bf16[512,2048]{1,0:T(8,128)(2,1)} %all-gather.3.cloned.1.call-done, bf16[2048,6656]{1,0:T(8,128)(2,1)} %param.6), kind=kOutput, calls=%fused_computation | convolution fusion | flops 13962051584 | bytes 36175872 | tf_op jit(solution)/shard_map/dot_general | solution.py:17
  55.9 9.9 %copy.7 = bf16[512,6656]{0,1:T(8,128)(2,1)} copy(bf16[512,6656]{1,0:T(8,128)(2,1)} %convolution_convert_fusion) | data formatting | bytes 13631488
  65.9 0.0 copy-start
  65.9 0.0 reduce-scatter.12.cloned.1.call-update
  65.9 0.0 reduce-scatter.10.cloned.1.call-start
  66.0 1.5 copy-done
  67.5 21.4 %convolution_convert_fusion.1 = bf16[512,6656]{1,0:T(8,128)(2,1)} fusion(bf16[512,2048]{1,0:T(8,128)(2,1)S(1)} %copy-done, bf16[2048,6656]{1,0:T(8,128)(2,1)} %param.5), kind=kOutput, calls=%fused_computation.1 | convolution fusion | flops 13962051584 | bytes 36175872 | tf_op jit(solution)/shard_map/dot_general | solution.py:11
  88.8 10.0 %copy.5 = bf16[512,6656]{0,1:T(8,128)(2,1)} copy(bf16[512,6656]{1,0:T(8,128)(2,1)} %convolution_convert_fusion.1) | data formatting | bytes 13631488
  98.8 0.0 reduce-scatter.10.cloned.1.call-update
  98.8 0.2 all-gather.5.cloned.1.call-start
  99.0 86.3 %reduce-scatter.12.cloned.1.call-done = bf16[1664,512]{1,0:T(8,128)(2,1)} async-done(((bf16[6656,512]{1,0:T(8,128)(2,1)}), bf16[1664,512]{1,0:T(8,128)(2,1)}) %reduce-scatter.12.cloned.1.call-update) | async-done | bytes 1703952
  185.3 2.7 copy.8
  188.1 119.3 %reduce-scatter.10.cloned.1.call-done = bf16[1664,512]{1,0:T(8,128)(2,1)} async-done(((bf16[6656,512]{1,0:T(8,128)(2,1)}), bf16[1664,512]{1,0:T(8,128)(2,1)}) %reduce-scatter.10.cloned.1.call-update) | async-done | bytes 1703952
  307.4 2.7 copy.6
  310.2 2.3 fusion.4
  312.4 0.0 all-gather.5.cloned.1.call-update
  312.4 0.0 reduce-scatter.8.cloned.1.call-start
  312.5 124.5 %all-gather.5.cloned.1.call-done = bf16[512,6656]{1,0:T(8,128)(2,1)} async-done(((bf16[512,1664]{1,0:T(8,128)(2,1)}), bf16[512,6656]{1,0:T(8,128)(2,1)}) %all-gather.5.cloned.1.call-update) | async-done | bytes 6815760 | tf_op jit(solution)/shard_map/all_gather | solution.py:25
  437.0 22.3 %convolution_convert_fusion.2 = bf16[512,2048]{1,0:T(8,128)(2,1)} fusion(bf16[512,6656]{1,0:T(8,128)(2,1)} %all-gather.5.cloned.1.call-done, bf16[6656,2048]{1,0:T(8,128)(2,1)} %param.7), kind=kOutput, calls=%fused_computation.9 | convolution fusion | flops 13959692288 | bytes 36175872 | tf_op jit(solution)/shard_map/dot_general | solution.py:24
  459.3 0.0 reduce-scatter.8.cloned.1.call-update
  459.3 29.8 %reduce-scatter.8.cloned.1.call-done = bf16[512,512]{1,0:T(8,128)(2,1)} async-done(((bf16[512,2048]{1,0:T(8,128)(2,1)}), bf16[512,512]{1,0:T(8,128)(2,1)}) %reduce-scatter.8.cloned.1.call-update) | async-done | bytes 524304 | tf_op jit(solution)/shard_map/reduce_scatter | solution.py:29
Async XLA Ops:
  6.5 27.7 %all-gather.3.cloned.1.call-start = ((), (), s32[]{:S(2)}) async-start(), calls=%async_computation.3 | async-start | bytes 2621440 | tf_op jit(solution)/shard_map/all_gather | solution.py:8
  7.3 178.1 %reduce-scatter.12.cloned.1.call-start = ((), (), s32[]{:S(2)}) async-start(), calls=%async_computation.7 | async-start | bytes 8519680
  65.9 1.6 copy-start
  65.9 241.5 %reduce-scatter.10.cloned.1.call-start = ((), (), s32[]{:S(2)}) async-start(), calls=%async_computation.6 | async-start | bytes 8519680
  98.8 338.2 %all-gather.5.cloned.1.call-start = ((), (), s32[]{:S(2)}) async-start(), calls=%async_computation.4 | async-start | bytes 8519680 | tf_op jit(solution)/shard_map/all_gather | solution.py:25
  312.4 176.6 %reduce-scatter.8.cloned.1.call-start = ((), (), s32[]{:S(2)}) async-start(), calls=%async_computation.5 | async-start | bytes 2621440 | tf_op jit(solution)/shard_map/reduce_scatter | solution.py:29
Sparse Core Ops, SparseCore 0:
  8.9 25.2 all-gather.2
  66.0 119.2 reduce-scatter.11
  187.6 119.7 reduce-scatter.9
  312.6 124.4 all-gather.4
  459.4 29.5 reduce-scatter.7
where the time goes:
time: 496 us
  waiting for transfers between devices  388 us (78%)
  matrix products  65.3 us (13%)
  local copies, waits for them, and re-layouts  26.9 us (5%)
  between operations  13.2 us (3%)
    unnamed x7, waiting for transfers between devices  206 us
    all_gather x1, waiting for transfers between devices, body(): lax.all_gather(hidden, 'gx', axis=1, tiled=True)  125 us
    reduce_scatter x1, waiting for transfers between devices, body(): lax.psum_scatter(projected.astype(jnp.bfloat16), ('gy', 'gz'), scatter_di...  29.8 us
    all_gather x1, waiting for transfers between devices, body(): features = lax.all_gather(tokens, ('gy', 'gz'), axis=1, tiled=True)  26.9 us
    unnamed x6, local copies, waits for them, and re-layouts  26.9 us
    dot_general x1, matrix products, body(): jnp.dot(lax.all_gather(hidden, 'gx', axis=1, tiled=True), down_weight, pr...  22.3 us
    dot_general x1, matrix products, body(): jnp.dot(features, up_weight, preferred_element_type=jnp.float32)  21.7 us
    dot_general x1, matrix products, body(): jnp.dot(features, gate_weight, preferred_element_type=jnp.float32)  21.4 us
  transfers between devices with their start and end apart: 5, of which 5 were waited for; matrix products, arithmetic and copies ran while one was open for 7% of the time, Pallas kernels for 0%

commit v1 on v0

v1 whole, which is shorter than its diff:
```python
import functools

import jax
import jax.numpy as jnp
from jax import lax
from jax.experimental import pallas as pl
from jax.experimental.pallas import tpu as pltpu
from jax.sharding import PartitionSpec as P

MESH = pl.DeviceIdType.MESH
WIDE = 128
LAG = 2
F32, BF16 = jnp.float32, jnp.bfloat16


def both(low, value, high):
    return jnp.logical_and(value >= low, value < high)


def kernel(
    n, count, pair, tok, gate, up, down, out,
    part, got, hid, acc, wbuf, dbuf,
    psend, precv, hsend, hrecv, wsem, dsem,
):
    z = lax.axis_index("gx")
    half = count * WIDE
    base = max(count, n - 1 + LAG)
    hop = (n - 1 - z, z)
    below, above = jnp.maximum(z - 1, 0), jnp.minimum(z + 1, n - 1)
    sum_to, hid_to = (below, above), (above, below)

    barrier = pltpu.get_barrier_semaphore()

    @pl.when(z > 0)
    def _():
        pl.semaphore_signal(barrier, inc=1, device_id={"gx": below}, device_id_type=MESH)

    @pl.when(z < n - 1)
    def _():
        pl.semaphore_signal(barrier, inc=1, device_id={"gx": above}, device_id_type=MESH)

    pl.semaphore_wait(barrier, jnp.minimum(z, 1) + jnp.minimum(n - 1 - z, 1))

    def weights(d, c, slot):
        columns = pl.ds(pl.multiple_of(d * half + c * WIDE, WIDE), WIDE)
        return [
            pltpu.make_async_copy(
                w.at[:, columns], wbuf.at[slot, d, :, pl.ds(i * WIDE, WIDE)], wsem.at[slot, d, i]
            )
            for i, w in enumerate((gate, up))
        ]

    def downs(d, q, slot):
        rows = pl.ds(pl.multiple_of(d * half + q * pair * WIDE, WIDE), pair * WIDE)
        return pltpu.make_async_copy(down.at[rows, :], dbuf.at[slot, d], dsem.at[slot, d])

    def sums(d, c):
        return pltpu.make_async_remote_copy(
            src_ref=part.at[d, c], dst_ref=got.at[d, c],
            send_sem=psend.at[d, lax.rem(c, 2)], recv_sem=precv.at[d, c],
            device_id={"gx": sum_to[d]}, device_id_type=MESH,
        )

    def hiddens(d, c):
        return pltpu.make_async_remote_copy(
            src_ref=hid.at[d, c], dst_ref=hid.at[d, c],
            send_sem=hsend.at[d, lax.rem(c, 2)], recv_sem=hrecv.at[d, c],
            device_id={"gx": hid_to[d]}, device_id_type=MESH,
        )

    def send(make, d, c):
        @pl.when(c >= 2)
        def _():
            make(d, c - 2).wait_send()

        make(d, c).start()

    def multiply(c):
        slot = lax.rem(c, 2)
        for d in range(2):
            for copy in weights(d, c, slot):
                copy.wait()
            part[d, c] = jnp.dot(
                tok[...], wbuf[slot, d], preferred_element_type=F32
            ).astype(BF16)

            @pl.when(c + 2 < count)
            def _():
                for copy in weights(d, c + 2, slot):
                    copy.start()

    for d in range(2):
        for c in range(min(2, count)):
            for copy in weights(d, c, c):
                copy.start()
    for d in range(2):
        for q in range(min(2, count // pair)):
            downs(d, q, q).start()
    acc[...] = jnp.zeros_like(acc)
    multiply(jnp.int32(0))

    def step(t, carry):
        for d in range(2):
            @pl.when(jnp.logical_and(hop[d] == 0, t < count))
            def _():
                send(sums, d, t)

        @pl.when(t + 1 < count)
        def _():
            multiply(t + 1)

        for d in range(2):
            c = t - hop[d]

            @pl.when(jnp.logical_and(both(1, hop[d], n - 1), both(0, c, count)))
            def _():
                sums(d, c).wait_recv()
                part[d, c] = (part[d, c].astype(F32) + got[d, c].astype(F32)).astype(BF16)
                send(sums, d, c)

        for d in range(2):
            c = t - (n - 1) - LAG

            @pl.when(jnp.logical_and(hop[d] == n - 1, both(0, c, count)))
            def _():
                sums(d, c).wait_recv()
                total = part[d, c].astype(F32) + got[d, c].astype(F32)
                g, u = total[:, :WIDE], total[:, WIDE:]
                hid[d, c] = (g / (1.0 + jnp.exp(-g)) * u).astype(BF16)

        for d in range(2):
            away = n - 1 - hop[d]
            c = t - base - away
            live = both(0, c, count)

            @pl.when(jnp.logical_and(away > 0, live))
            def _():
                hiddens(d, c).wait_recv()

            @pl.when(jnp.logical_and(away < n - 1, live))
            def _():
                send(hiddens, d, c)

        for d in range(2):
            c = t - base - (n - 1 - hop[d])
            q = c // pair

            @pl.when(jnp.logical_and(both(0, c, count), lax.rem(c, pair) == pair - 1))
            def _():
                slot = lax.rem(q, 2)
                downs(d, q, slot).wait()
                units = jnp.concatenate([hid[d, q * pair + i] for i in range(pair)], axis=1)
                acc[...] += jnp.dot(units, dbuf[slot, d], preferred_element_type=F32)

                @pl.when(q + 2 < count // pair)
                def _():
                    downs(d, q + 2, slot).start()

        return carry

    lax.fori_loop(0, base + count + n - 1, step, 0)
    out[...] = acc[...].astype(BF16)

    for d in range(2):
        for c in range(max(0, count - 2), count):
            @pl.when(hop[d] < n - 1)
            def _():
                sums(d, jnp.int32(c)).wait_send()

            @pl.when(hop[d] > 0)
            def _():
                hiddens(d, jnp.int32(c)).wait_send()


def body(n, tokens, gate_weight, up_weight, down_weight):
    features = lax.all_gather(tokens, ("gy", "gz"), axis=1, tiled=True)
    rows, depth = features.shape
    columns, width = down_weight.shape
    count = columns // (2 * WIDE)
    pair = 2 if count % 2 == 0 else 1
    projected = pl.pallas_call(
        functools.partial(kernel, n, count, pair),
        out_shape=jax.ShapeDtypeStruct((rows, width), BF16),
        in_specs=[pl.BlockSpec(memory_space=pltpu.VMEM)] + [pl.BlockSpec(memory_space=pl.ANY)] * 3,
        out_specs=pl.BlockSpec(memory_space=pltpu.VMEM),
        scratch_shapes=[
            pltpu.VMEM((2, count, rows, 2 * WIDE), BF16),
            pltpu.VMEM((2, count, rows, 2 * WIDE), BF16),
            pltpu.VMEM((2, count, rows, WIDE), BF16),
            pltpu.VMEM((rows, width), F32),
            pltpu.VMEM((2, 2, depth, 2 * WIDE), BF16),
            pltpu.VMEM((2, 2, pair * WIDE, width), BF16),
            pltpu.SemaphoreType.DMA((2, 2)),
            pltpu.SemaphoreType.DMA((2, count)),
            pltpu.SemaphoreType.DMA((2, 2)),
            pltpu.SemaphoreType.DMA((2, count)),
            pltpu.SemaphoreType.DMA((2, 2, 2)),
            pltpu.SemaphoreType.DMA((2, 2)),
        ],
        compiler_params=pltpu.CompilerParams(
            collective_id=0, has_side_effects=True, vmem_limit_bytes=60 * 2**20
        ),
    )(features, gate_weight, up_weight, down_weight)
    return lax.psum_scatter(projected, ("gy", "gz"), scatter_dimension=1, tiled=True)


def solution(mesh):
    placed = (
        P("rep", ("gx", "gy", "gz")),
        P("gx", ("gy", "gz")),
        P("gx", ("gy", "gz")),
        P(("gy", "gz"), "gx"),
    )
    return jax.shard_map(
        functools.partial(body, mesh.shape["gx"]),
        mesh=mesh, in_specs=placed, out_specs=P("rep", ("gx", "gy", "gz")), check_vma=False,
    )
```

time: 496 us -> 346 us (0.70)
  waiting for transfers between devices: 388 us -> 56.5 us
  Pallas kernels: 0 us -> 276 us
  matrix products: 65.3 us -> 0 us
  local copies, waits for them, and re-layouts: 26.9 us -> 0 us
    pallas_call x0 -> x1, Pallas kernels: none -> 276 us  [body(): pl.pallas_call(functools.partial(kernel, n, count, pair), out_shape=jax.S...]
    unnamed x7 -> x2, waiting for transfers between devices: 206 us -> 0.73 us
    all_gather x1 -> x0, waiting for transfers between devices: 125 us -> none  [body(): lax.all_gather(hidden, 'gx', axis=1, tiled=True)]
    dot_general x3 -> x0, matrix products: 65.3 us -> none  [the longest x1 22.3 us: body(): jnp.dot(lax.all_gather(hidden, 'gx', axis=1, tiled=True), down_weight, pr...]
    unnamed x6 -> x0, local copies, waits for them, and re-layouts: 26.9 us -> none
  transfers between devices with their start and end apart: 5 -> 2, of which waited for: 5 -> 2; matrix products, arithmetic and copies ran while one was open for 7% -> 0% of each run, Pallas kernels for 0% -> 0%
where the time goes in v1:
time: 346 us
  Pallas kernels  276 us (80%)
  waiting for transfers between devices  56.5 us (16%)
  between operations  13.4 us (4%)
    pallas_call x1, Pallas kernels, body(): pl.pallas_call(functools.partial(kernel, n, count, pair), out_shape=jax.S...  276 us
    reduce_scatter x1, waiting for transfers between devices, body(): lax.psum_scatter(projected, ('gy', 'gz'), scatter_dimension=1, tiled=True)  28.8 us
    all_gather x1, waiting for transfers between devices, body(): features = lax.all_gather(tokens, ('gy', 'gz'), axis=1, tiled=True)  26.9 us
  transfers between devices with their start and end apart: 2, of which 2 were waited for; matrix products, arithmetic and copies ran while one was open for 0% of the time, Pallas kernels for 0%

profile of v1, /device:TPU:0, one launch (start us, length us, event | category | flops | bytes accessed | tf_op | source)
XLA Modules:
  0.0 346.0 jit_solution(13720678775372936300)
XLA Ops:
  6.5 0.0 all-gather.2.cloned.1.call-start
  6.5 0.7 all-gather.2.cloned.1.call-update
  7.3 0.0 reduce-scatter.2.cloned.1.call-start
  7.3 26.9 %all-gather.2.cloned.1.call-done.tok = bf16[512,2048]{1,0:T(8,128)(2,1)} async-done(((bf16[512,512]{1,0:T(8,128)(2,1)}), bf16[512,2048]{1,0:T(8,128)(2,1)}) %all-gather.2.cloned.1.call-update) | async-done | bytes 2097168 | tf_op jit(solution)/shard_map/all_gather | solution.py:176
  34.2 276.0 %shard_map.46 = bf16[512,2048]{1,0:T(8,128)(2,1)} custom-call(bf16[512,2048]{1,0:T(8,128)(2,1)} %all-gather.2.cloned.1.call-done.tok, bf16[2048,6656]{1,0:T(8,128)(2,1)} %gate.1, bf16[2048,6656]{1,0:T(8,128)(2,1)} %up.1, bf16[6656,2048]{1,0:T(8,128)(2,1)} %down.1), custom_call_target="tpu_custom_call" | custom-call | tf_op jit(solution)/shard_map/pallas_call | solution.py:181
  310.3 0.0 reduce-scatter.2.cloned.1.call-update
  310.3 28.8 %reduce-scatter.2.cloned.1.call-done = bf16[512,512]{1,0:T(8,128)(2,1)} async-done(((bf16[512,2048]{1,0:T(8,128)(2,1)}), bf16[512,512]{1,0:T(8,128)(2,1)}) %reduce-scatter.2.cloned.1.call-update) | async-done | bytes 524304 | tf_op jit(solution)/shard_map/reduce_scatter | solution.py:204
Async XLA Ops:
  6.5 27.7 %all-gather.2.cloned.1.call-start = ((), (), s32[]{:S(2)}) async-start(), calls=%async_computation.1 | async-start | bytes 2621440 | tf_op jit(solution)/shard_map/all_gather | solution.py:176
  7.3 331.9 %reduce-scatter.2.cloned.1.call-start = ((), (), s32[]{:S(2)}) async-start(), calls=%async_computation.2 | async-start | bytes 2621440 | tf_op jit(solution)/shard_map/reduce_scatter | solution.py:204
Sparse Core Ops, SparseCore 0:
  8.9 25.2 all-gather.1
  310.4 28.6 reduce-scatter.1

commit v2 on v1

v2 whole, which is shorter than its diff:
```python
import functools

import jax
import jax.numpy as jnp
from jax import lax
from jax.experimental import pallas as pl
from jax.experimental.pallas import tpu as pltpu
from jax.sharding import PartitionSpec as P

MESH = pl.DeviceIdType.MESH
WIDE = 128
LAG = 4
FLIGHT = 4
PARTS = 2
F32, BF16 = jnp.float32, jnp.bfloat16


def both(low, value, high):
    return jnp.logical_and(value >= low, value < high)


def kernel(
    n, ny, nz, count, pair, fused, own, gate, up, down, out,
    tok, part, got, hid, acc, wbuf, dbuf, core_out, core_in, chip_out, chip_in,
    psend, precv, hsend, hrecv, wsem, dsem,
    tok_chip_send, tok_chip_recv, tok_core_send, tok_core_recv,
    core_send, core_recv, chip_send, chip_recv,
):
    z, y, k = lax.axis_index("gx"), lax.axis_index("gy"), lax.axis_index("gz")
    rows = acc.shape[0] // PARTS
    half = count * WIDE
    pairs = count // pair
    units, hunits = PARTS * count, PARTS * pairs
    ready = [(v // pairs) * count + (v % pairs + 1) * pair - 1 + n - 1 + LAG - v for v in range(hunits)]
    base = max([units] + ready)
    steps = base + hunits + n - 1
    hop = (n - 1 - z, z)
    below, above = jnp.maximum(z - 1, 0), jnp.minimum(z + 1, n - 1)
    sum_to, hid_to = (below, above), (above, below)

    barrier = pltpu.get_barrier_semaphore()

    @pl.when(z > 0)
    def _():
        pl.semaphore_signal(barrier, inc=1, device_id={"gx": below}, device_id_type=MESH)

    @pl.when(z < n - 1)
    def _():
        pl.semaphore_signal(barrier, inc=1, device_id={"gx": above}, device_id_type=MESH)

    others = 0
    if fused:
        for j in range(1, ny):
            pl.semaphore_signal(barrier, inc=1, device_id={"gy": lax.rem(y + j, ny)}, device_id_type=MESH)
        for i in range(1, nz):
            pl.semaphore_signal(barrier, inc=1, device_id={"gz": lax.rem(k + i, nz)}, device_id_type=MESH)
        others = ny + nz - 2

    def weights(d, u, slot):
        columns = pl.ds(pl.multiple_of(d * half + lax.rem(u, count) * WIDE, WIDE), WIDE)
        return [
            pltpu.make_async_copy(
                w.at[:, columns], wbuf.at[slot, d, :, pl.ds(i * WIDE, WIDE)], wsem.at[slot, d, i]
            )
            for i, w in enumerate((gate, up))
        ]

    def downs(d, v, slot):
        q = lax.rem(v, pairs)
        units_of = pl.ds(pl.multiple_of(d * half + q * pair * WIDE, WIDE), pair * WIDE)
        return pltpu.make_async_copy(down.at[units_of, :], dbuf.at[slot, d], dsem.at[slot, d])

    def sums(d, u):
        return pltpu.make_async_remote_copy(
            src_ref=part.at[d, u], dst_ref=got.at[d, u],
            send_sem=psend.at[d, lax.rem(u, FLIGHT)], recv_sem=precv.at[d, u],
            device_id={"gx": sum_to[d]}, device_id_type=MESH,
        )

    def hiddens(d, v):
        block = hid.at[d, pl.ds(v * pair, pair)]
        return pltpu.make_async_remote_copy(
            src_ref=block, dst_ref=block,
            send_sem=hsend.at[d, lax.rem(v, FLIGHT)], recv_sem=hrecv.at[d, v],
            device_id={"gx": hid_to[d]}, device_id_type=MESH,
        )

    def send(make, d, u):
        @pl.when(u >= FLIGHT)
        def _():
            make(d, u - FLIGHT).wait_send()

        make(d, u).start()

    def rows_of(r):
        return pl.ds(r * rows, rows)

    def block_of(yy, kk):
        width = own.shape[1]
        return pl.ds(pl.multiple_of((yy * nz + kk) * width, WIDE), width)

    def tok_chip(r, j):
        return pltpu.make_async_remote_copy(
            src_ref=own.at[rows_of(r), :], dst_ref=tok.at[rows_of(r), block_of(y, k)],
            send_sem=tok_chip_send.at[r, j], recv_sem=tok_chip_recv.at[r, j],
            device_id={"gy": lax.rem(y + j, ny)}, device_id_type=MESH,
        )

    def tok_core(r, i, j):
        block = tok.at[rows_of(r), block_of(lax.rem(y + ny - j, ny), k)]
        return pltpu.make_async_remote_copy(
            src_ref=own.at[rows_of(r), :] if j == 0 else block, dst_ref=block,
            send_sem=tok_core_send.at[r, i, j], recv_sem=tok_core_recv.at[r, i, j],
            device_id={"gz": lax.rem(k + i, nz)}, device_id_type=MESH,
        )

    def tok_start():
        for r in range(PARTS):
            for j in range(1, ny):
                tok_chip(r, j).start()
        for r in range(PARTS):
            for i in range(1, nz):
                tok_core(r, i, 0).start()
        tok[:, block_of(y, k)] = own[...]

    def tok_hand_on(r):
        for j in range(1, ny):
            tok_chip(r, j).wait_recv()
            for i in range(1, nz):
                tok_core(r, i, j).start()

    def tok_finish(r):
        for i in range(1, nz):
            for j in range(ny):
                tok_core(r, i, j).wait_recv()
        for j in range(1, ny):
            tok_chip(r, j).wait_send()
        for i in range(1, nz):
            for j in range(ny):
                tok_core(r, i, j).wait_send()

    def out_block(yy, kk):
        width = out.shape[1]
        return pl.ds(pl.multiple_of((yy * nz + kk) * width, WIDE), width)

    def core_copy(r, i):
        return pltpu.make_async_remote_copy(
            src_ref=core_out.at[r, i - 1], dst_ref=core_in.at[r, i - 1],
            send_sem=core_send.at[r, i], recv_sem=core_recv.at[r, i],
            device_id={"gz": lax.rem(k + i, nz)}, device_id_type=MESH,
        )

    def chip_copy(r, j):
        return pltpu.make_async_remote_copy(
            src_ref=chip_out.at[r, j - 1], dst_ref=chip_in.at[r, j - 1],
            send_sem=chip_send.at[r, j], recv_sem=chip_recv.at[r, j],
            device_id={"gy": lax.rem(y + j, ny)}, device_id_type=MESH,
        )

    def out_cores(r):
        for i in range(1, nz):
            for yy in range(ny):
                core_out[r, i - 1, yy] = acc[rows_of(r), out_block(yy, lax.rem(k + i, nz))].astype(BF16)
            core_copy(r, i).start()

    def chip_sum(r, yy):
        total = acc[rows_of(r), out_block(yy, k)]
        for i in range(1, nz):
            total += core_in[r, i - 1, yy].astype(F32)
        return total

    def out_chips(r):
        for i in range(1, nz):
            core_copy(r, i).wait()
        for j in range(1, ny):
            chip_out[r, j - 1] = chip_sum(r, lax.rem(y + j, ny)).astype(BF16)
            chip_copy(r, j).start()

    def out_finish(r):
        total = chip_sum(r, y)
        for j in range(1, ny):
            chip_copy(r, j).wait()
            total += chip_in[r, j - 1].astype(F32)
        out[rows_of(r), :] = total.astype(BF16)

    features = tok if fused else own

    def multiply(u):
        slot = lax.rem(u, 2)
        first = pl.multiple_of((u // count) * rows, rows)
        for d in range(2):
            for copy in weights(d, u, slot):
                copy.wait()
            part[d, u] = jnp.dot(
                features[pl.ds(first, rows), :], wbuf[slot, d], preferred_element_type=F32
            ).astype(BF16)

            @pl.when(u + 2 < units)
            def _():
                for copy in weights(d, u + 2, slot):
                    copy.start()

    for c in range(2):
        for d in range(2):
            for copy in weights(d, jnp.int32(c), c):
                copy.start()
    for d in range(2):
        for v in range(2):
            downs(d, jnp.int32(v), v).start()
    pl.semaphore_wait(barrier, jnp.minimum(z, 1) + jnp.minimum(n - 1 - z, 1) + others)
    if fused:
        tok_start()
        acc[...] = jnp.zeros_like(acc)
        tok_hand_on(0)
        tok_finish(0)
    else:
        acc[...] = jnp.zeros_like(acc)
    multiply(jnp.int32(0))

    def step(t, carry):
        for d in range(2):
            @pl.when(jnp.logical_and(hop[d] == 0, t < units))
            def _():
                send(sums, d, t)

        if fused:
            for r in range(1, PARTS):
                @pl.when(t == min(4, count - 2))
                def _():
                    tok_hand_on(r)

                @pl.when(t == min(8, count - 2))
                def _():
                    tok_finish(r)

        @pl.when(t + 1 < units)
        def _():
            multiply(t + 1)

        for d in range(2):
            u = t - hop[d]

            @pl.when(jnp.logical_and(both(1, hop[d], n - 1), both(0, u, units)))
            def _():
                sums(d, u).wait_recv()
                part[d, u] = (part[d, u].astype(F32) + got[d, u].astype(F32)).astype(BF16)
                send(sums, d, u)

        for d in range(2):
            u = t - (n - 1) - LAG

            @pl.when(jnp.logical_and(hop[d] == n - 1, both(0, u, units)))
            def _():
                sums(d, u).wait_recv()
                total = part[d, u].astype(F32) + got[d, u].astype(F32)
                g, w = total[:, :WIDE], total[:, WIDE:]
                hid[d, u] = (g / (1.0 + jnp.exp(-g)) * w).astype(BF16)

        for d in range(2):
            away = n - 1 - hop[d]
            v = t - base - away
            live = both(0, v, hunits)

            @pl.when(jnp.logical_and(away > 0, live))
            def _():
                hiddens(d, v).wait_recv()

            @pl.when(jnp.logical_and(away < n - 1, live))
            def _():
                send(hiddens, d, v)

            @pl.when(live)
            def _():
                slot = lax.rem(v, 2)
                downs(d, v, slot).wait()
                first = pl.ds(pl.multiple_of((v // pairs) * rows, rows), rows)
                block = jnp.concatenate([hid[d, v * pair + i] for i in range(pair)], axis=1)
                acc[first, :] += jnp.dot(block, dbuf[slot, d], preferred_element_type=F32)

                @pl.when(v + 2 < hunits)
                def _():
                    downs(d, v + 2, slot).start()

        if fused:
            for r in range(PARTS - 1):
                whole = base + (r + 1) * pairs - 1 + n - 1
                for stage, after in ((out_cores, 0), (out_chips, 2), (out_finish, 6)):
                    @pl.when(t == min(whole + after, steps - 1))
                    def _():
                        stage(r)

        return carry

    lax.fori_loop(0, steps, step, 0)
    if fused:
        for stage in (out_cores, out_chips, out_finish):
            stage(PARTS - 1)
    else:
        out[...] = acc[...].astype(BF16)

    for d in range(2):
        @pl.when(hop[d] < n - 1)
        def _():
            for u in range(units - FLIGHT, units):
                sums(d, jnp.int32(u)).wait_send()

        @pl.when(hop[d] > 0)
        def _():
            for v in range(hunits - FLIGHT, hunits):
                hiddens(d, jnp.int32(v)).wait_send()


def body(n, ny, nz, tokens, gate_weight, up_weight, down_weight):
    depth = gate_weight.shape[0]
    columns, width = down_weight.shape
    fused = tokens.shape[1] % WIDE == 0 and width % (ny * nz * WIDE) == 0
    if not fused:
        tokens = lax.all_gather(tokens, ("gy", "gz"), axis=1, tiled=True)
    rows = tokens.shape[0]
    own_width = width // (ny * nz) if fused else width
    count = columns // (2 * WIDE)
    pair = 2 if count % 2 == 0 else 1
    units, part_rows = PARTS * count, rows // PARTS
    dma = pltpu.SemaphoreType.DMA
    result = pl.pallas_call(
        functools.partial(kernel, n, ny, nz, count, pair, fused),
        out_shape=jax.ShapeDtypeStruct((rows, own_width), BF16),
        in_specs=[pl.BlockSpec(memory_space=pltpu.VMEM)] + [pl.BlockSpec(memory_space=pl.ANY)] * 3,
        out_specs=pl.BlockSpec(memory_space=pltpu.VMEM),
        scratch_shapes=[
            pltpu.VMEM((rows, depth) if fused else (16, WIDE), BF16),
            pltpu.VMEM((2, units, part_rows, 2 * WIDE), BF16),
            pltpu.VMEM((2, units, part_rows, 2 * WIDE), BF16),
            pltpu.VMEM((2, units, part_rows, WIDE), BF16),
            pltpu.VMEM((rows, width), F32),
            pltpu.VMEM((2, 2, depth, 2 * WIDE), BF16),
            pltpu.VMEM((2, 2, pair * WIDE, width), BF16),
            *[
                pltpu.VMEM(shape if fused else (16, WIDE), BF16)
                for shape in [(PARTS, nz - 1, ny, part_rows, own_width)] * 2
                + [(PARTS, ny - 1, part_rows, own_width)] * 2
            ],
            dma((2, FLIGHT)), dma((2, units)), dma((2, FLIGHT)), dma((2, units // pair)),
            dma((2, 2, 2)), dma((2, 2)),
            dma((PARTS, ny)), dma((PARTS, ny)), dma((PARTS, nz, ny)), dma((PARTS, nz, ny)),
            dma((PARTS, nz)), dma((PARTS, nz)), dma((PARTS, ny)), dma((PARTS, ny)),
        ],
        compiler_params=pltpu.CompilerParams(
            collective_id=0, has_side_effects=True, vmem_limit_bytes=60 * 2**20
        ),
    )(tokens, gate_weight, up_weight, down_weight)
    if fused:
        return result
    return lax.psum_scatter(result, ("gy", "gz"), scatter_dimension=1, tiled=True)


def solution(mesh):
    placed = (
        P("rep", ("gx", "gy", "gz")),
        P("gx", ("gy", "gz")),
        P("gx", ("gy", "gz")),
        P(("gy", "gz"), "gx"),
    )
    return jax.shard_map(
        functools.partial(body, mesh.shape["gx"], mesh.shape["gy"], mesh.shape["gz"]),
        mesh=mesh, in_specs=placed, out_specs=P("rep", ("gx", "gy", "gz")), check_vma=False,
    )
```

time: 346 us -> 336 us (0.971)
  Pallas kernels: 276 us -> 334 us
  waiting for transfers between devices: 56.5 us -> 0 us
  between operations: 13.4 us -> 0.01 us
    pallas_call x1, Pallas kernels: 276 us -> 334 us  [body(): pl.pallas_call(functools.partial(kernel, n, ny, nz, count, pair, fused),...]
    reduce_scatter x1 -> x0, waiting for transfers between devices: 28.8 us -> none  [body(): lax.psum_scatter(projected, ('gy', 'gz'), scatter_dimension=1, tiled=True)]
    all_gather x1 -> x0, waiting for transfers between devices: 26.9 us -> none  [body(): features = lax.all_gather(tokens, ('gy', 'gz'), axis=1, tiled=True)]
  transfers between devices with their start and end apart: 2 -> 0, of which waited for: 2 -> 0; matrix products, arithmetic and copies ran while one was open for 0% -> 0% of each run, Pallas kernels for 0% -> 0%
where the time goes in v2:
time: 336 us
  Pallas kernels  334 us (99%)
    pallas_call x1, Pallas kernels, body(): pl.pallas_call(functools.partial(kernel, n, ny, nz, count, pair, fused),...  334 us

profile of v2, /device:TPU:0, one launch (start us, length us, event | category | flops | bytes accessed | tf_op | source)
XLA Modules:
  0.0 336.2 jit_solution(5309095672363506111)
XLA Ops:
  0.0 334.3 %shard_map.46 = bf16[512,512]{1,0:T(8,128)(2,1)} custom-call(bf16[512,512]{1,0:T(8,128)(2,1)} %own.1, bf16[2048,6656]{1,0:T(8,128)(2,1)} %gate.1, bf16[2048,6656]{1,0:T(8,128)(2,1)} %up.1, bf16[6656,2048]{1,0:T(8,128)(2,1)} %down.1), custom_call_target="tpu_custom_call" | custom-call | tf_op jit(solution)/shard_map/pallas_call | solution.py:325
  334.4 1.9 copy.6

commit v3 on v2

--- a/solution.py
+++ b/solution.py
@@ -9,7 +9,8 @@
 
 MESH = pl.DeviceIdType.MESH
 WIDE = 128
-LAG = 4
+LAG = 2
+SPACE = 3
 FLIGHT = 4
 PARTS = 2
 F32, BF16 = jnp.float32, jnp.bfloat16
@@ -31,9 +32,9 @@
     half = count * WIDE
     pairs = count // pair
     units, hunits = PARTS * count, PARTS * pairs
-    ready = [(v // pairs) * count + (v % pairs + 1) * pair - 1 + n - 1 + LAG - v for v in range(hunits)]
+    ready = [(v // pairs) * count + (v % pairs + 1) * pair - 1 + SPACE * (n - 1) + LAG - v for v in range(hunits)]
     base = max([units] + ready)
-    steps = base + hunits + n - 1
+    steps = base + hunits + SPACE * (n - 1)
     hop = (n - 1 - z, z)
     below, above = jnp.maximum(z - 1, 0), jnp.minimum(z + 1, n - 1)
     sum_to, hid_to = (below, above), (above, below)
@@ -238,7 +239,7 @@
             multiply(t + 1)
 
         for d in range(2):
-            u = t - hop[d]
+            u = t - SPACE * hop[d]
 
             @pl.when(jnp.logical_and(both(1, hop[d], n - 1), both(0, u, units)))
             def _():
@@ -247,7 +248,7 @@
                 send(sums, d, u)
 
         for d in range(2):
-            u = t - (n - 1) - LAG
+            u = t - SPACE * (n - 1) - LAG
 
             @pl.when(jnp.logical_and(hop[d] == n - 1, both(0, u, units)))
             def _():
@@ -258,7 +259,7 @@
 
         for d in range(2):
             away = n - 1 - hop[d]
-            v = t - base - away
+            v = t - base - SPACE * away
             live = both(0, v, hunits)
 
             @pl.when(jnp.logical_and(away > 0, live))
@@ -283,7 +284,7 @@
 
         if fused:
             for r in range(PARTS - 1):
-                whole = base + (r + 1) * pairs - 1 + n - 1
+                whole = base + (r + 1) * pairs - 1 + SPACE * (n - 1)
                 for stage, after in ((out_cores, 0), (out_chips, 2), (out_finish, 6)):
                     @pl.when(t == min(whole + after, steps - 1))
                     def _():

time: 336 us -> 264 us (0.79)
  Pallas kernels: 334 us -> 262 us
    pallas_call x1, Pallas kernels: 334 us -> 262 us  [body(): pl.pallas_call(functools.partial(kernel, n, ny, nz, count, pair, fused),...]
where the time goes in v3:
time: 264 us
  Pallas kernels  262 us (99%)
    pallas_call x1, Pallas kernels, body(): pl.pallas_call(functools.partial(kernel, n, ny, nz, count, pair, fused),...  262 us

profile of v3, /device:TPU:0, one launch (start us, length us, event | category | flops | bytes accessed | tf_op | source)
XLA Modules:
  0.0 264.2 jit_solution(1991801385853358687)
XLA Ops:
  0.0 262.3 %shard_map.46 = bf16[512,512]{1,0:T(8,128)(2,1)} custom-call(bf16[512,512]{1,0:T(8,128)(2,1)} %own.1, bf16[2048,6656]{1,0:T(8,128)(2,1)} %gate.1, bf16[2048,6656]{1,0:T(8,128)(2,1)} %up.1, bf16[6656,2048]{1,0:T(8,128)(2,1)} %down.1), custom_call_target="tpu_custom_call" | custom-call | tf_op jit(solution)/shard_map/pallas_call | solution.py:326
  262.3 1.9 copy.6

commit v4 on v3

--- a/solution.py
+++ b/solution.py
@@ -10,7 +10,7 @@
 MESH = pl.DeviceIdType.MESH
 WIDE = 128
 LAG = 2
-SPACE = 3
+SPACE = 2
 FLIGHT = 4
 PARTS = 2
 F32, BF16 = jnp.float32, jnp.bfloat16

time: 264 us -> 262 us (level)
  Pallas kernels: 262 us -> 259 us
    pallas_call x1, Pallas kernels: 262 us -> 259 us  [body(): pl.pallas_call(functools.partial(kernel, n, ny, nz, count, pair, fused),...]
where the time goes in v4:
time: 262 us; the launch traced here: 261 us
  Pallas kernels  259 us (99%)
    pallas_call x1, Pallas kernels, body(): pl.pallas_call(functools.partial(kernel, n, ny, nz, count, pair, fused),...  259 us

profile of v4, /device:TPU:0, one launch (start us, length us, event | category | flops | bytes accessed | tf_op | source)
XLA Modules:
  0.0 261.4 jit_solution(8911687876582383699)
XLA Ops:
  0.0 259.5 %shard_map.46 = bf16[512,512]{1,0:T(8,128)(2,1)} custom-call(bf16[512,512]{1,0:T(8,128)(2,1)} %own.1, bf16[2048,6656]{1,0:T(8,128)(2,1)} %gate.1, bf16[2048,6656]{1,0:T(8,128)(2,1)} %up.1, bf16[6656,2048]{1,0:T(8,128)(2,1)} %down.1), custom_call_target="tpu_custom_call" | custom-call | tf_op jit(solution)/shard_map/pallas_call | solution.py:326
  259.5 1.9 copy.6
